TPU v7x, 1024 devices: a whole 4x4x32 slice. The times are simulated.
1024 devices in a mesh: dp: 64 (over z, core), tensor: 16 (over y, x).
Axes of the slice: x: 4, y: 4, z: 32, core: 2. Of those that a mesh axis runs over, the one named last changes fastest.
Arguments:
- acts: bfloat16 [16384, 4096], P(('dp', 'tensor')), may hold values from -6 to 6
- out_grad: bfloat16 [16384, 16384], P('dp', 'tensor'), may hold values from -0.375 to 0.375
- q_prev: bfloat16 [64, 16384], P(None, 'tensor'), may hold values from -0.046875 to 0.046875
Outputs:
- basis: float32 [64, 4096], replicated
- factor: float32 [64, 16384], P(None, 'tensor')
All inputs are finite; a program needn't handle non-finite values.
Results may differ from a plain program's by a relative error of at most 0.0041.
Values may be sent and summed in bfloat16 or wider, within the bound.
A program may use at most 32 MiB of HBM per device.

v0:
```python
import jax
import jax.numpy as jnp
from jax import lax
from jax.sharding import PartitionSpec as P


def shards(acts, out_grad, q_prev):
    replicas = lax.axis_size("dp")
    product = jnp.einsum(
        "tr,tf->rf",
        lax.all_gather(acts, "tensor", axis=0, tiled=True),
        out_grad,
        preferred_element_type=jnp.float32,
    )
    grads = product.astype(jnp.bfloat16)
    left_term = jnp.einsum("kf,rf->kr", q_prev, grads, preferred_element_type=jnp.float32)
    summed = lax.psum(left_term, ("dp", "tensor"))
    gram = jnp.dot(summed, summed.T, precision=lax.Precision.HIGHEST)
    lower = jnp.linalg.cholesky(gram)
    basis = lax.linalg.triangular_solve(lower, summed, left_side=True, lower=True)
    low = basis.astype(jnp.bfloat16)
    right_term = jnp.dot(low, grads, preferred_element_type=jnp.float32)
    factor = lax.psum(right_term, "dp") / replicas
    return (basis, factor)


def solution(mesh):
    in_specs = (P(("dp", "tensor"), None), P("dp", "tensor"), P(None, "tensor"))
    out_specs = (P(), P(None, "tensor"))
    return jax.shard_map(shards, mesh=mesh, in_specs=in_specs, out_specs=out_specs, check_vma=False)
```

profile of v0, /device:TPU:1, one launch (start us, length us, event | category | flops | bytes accessed | tf_op | source)
XLA Modules:
  0.0 1414.3 jit_solution(10192027593371460246)
XLA Ops:
  7.2 0.0 copy-start
  7.2 0.0 copy-start.3
  7.2 0.0 all-gather.2.cloned.1.call-start
  7.2 0.7 all-gather.2.cloned.1.call-update
  7.9 0.0 all-reduce.3.cloned.1.call-start
  8.0 92.6 %all-gather.2.cloned.1.call-done = bf16[256,4096]{1,0:T(8,128)(2,1)} async-done(((bf16[16,4096]{1,0:T(8,128)(2,1)}), bf16[256,4096]{1,0:T(8,128)(2,1)}) %all-gather.2.cloned.1.call-update) | async-done | bytes 2097168 | tf_op jit(solution)/shard_map/all_gather | solution.py:11
  100.5 0.0 copy-done
  100.5 4.0 convolution_convert_fusion
  104.5 0.0 copy-start.1
  104.5 3.2 copy-done.1
  107.7 0.0 copy-done.3
  107.7 3.6 convolution_bitcast_fusion
  111.4 0.0 all-reduce.3.cloned.1.call-update
  111.4 0.0 all-reduce.5.cloned.1.call-start
  111.4 892.1 %all-reduce.3.cloned.1.call-done = f32[64,4096]{1,0:T(8,128)} async-done(((f32[64,4096]{1,0:T(8,128)}), f32[64,4096]{1,0:T(8,128)}) %all-reduce.3.cloned.1.call-update) | async-done | bytes 1048592 | tf_op jit(solution)/shard_map/psum | solution.py:17
  1003.6 2.7 fusion.6
  1006.2 0.1 copy.5
  1006.3 5.8 cholesky.16
  1012.2 0.6 compare_reduce_fusion
  1012.9 0.7 fusion.2
  1013.5 4.9 custom-call.6
  1018.4 2.3 fusion.3
  1020.7 0.0 copy-start.2
  1020.7 6.0 fusion
  1026.7 0.0 copy-done.2
  1026.7 0.0 all-reduce.5.cloned.1.call-update
  1026.8 379.3 %all-reduce.5.cloned.1.call-done = f32[64,1024]{1,0:T(8,128)} async-done(((f32[64,1024]{1,0:T(8,128)}), f32[64,1024]{1,0:T(8,128)}) %all-reduce.5.cloned.1.call-update) | async-done | bytes 262160 | tf_op jit(solution)/shard_map/psum | solution.py:23
  1406.1 1.7 broadcast_multiply_fusion
  (2 shorter events, 0.0 us)
Async XLA Ops:
  7.2 93.4 %copy-start = (bf16[256,1024]{1,0:T(8,128)(2,1)S(1)}, bf16[256,1024]{1,0:T(8,128)(2,1)}, u32[]{:S(2)}) copy-start(bf16[256,1024]{1,0:T(8,128)(2,1)} %param.4) | copy-start | bytes 1572868
  7.2 100.6 %copy-start.3 = (bf16[64,1024]{1,0:T(8,128)(2,1)S(1)}, bf16[64,1024]{1,0:T(8,128)(2,1)}, u32[]{:S(2)}) copy-start(bf16[64,1024]{1,0:T(8,128)(2,1)} %param.5) | copy-start | bytes 393220
  7.2 93.3 %all-gather.2.cloned.1.call-start = ((), (), s32[]{:S(2)}) async-start(), calls=%async_computation | async-start | bytes 2228224 | tf_op jit(solution)/shard_map/all_gather | solution.py:11
  7.9 995.7 %all-reduce.3.cloned.1.call-start = ((), (), s32[]{:S(2)}) async-start(), calls=%async_computation.1 | async-start | bytes 2097152 | tf_op jit(solution)/shard_map/psum | solution.py:17
  104.5 3.2 copy-start.1
  111.4 1294.7 %all-reduce.5.cloned.1.call-start = ((), (), s32[]{:S(2)}) async-start(), calls=%async_computation.2 | async-start | bytes 524288 | tf_op jit(solution)/shard_map/psum | solution.py:23
  1020.7 6.0 copy-start.2
Sparse Core Ops, SparseCore 0:
  12.2 88.2 all-gather.1
  111.5 892.0 all-reduce.2
  1026.9 379.1 all-reduce.4
where the time goes:
time: 1410 us
  waiting for transfers between devices  1360 us (96%)
  matrix products  18.6 us (1%)
    psum x1, waiting for transfers between devices, shards(): summed = lax.psum(left_term, ('dp', 'tensor'))  892 us
    psum x1, waiting for transfers between devices, shards(): factor = lax.psum(right_term, 'dp') / replicas  379 us
    all_gather x1, waiting for transfers between devices, shards(): lax.all_gather(acts, 'tensor', axis=0, tiled=True)  92.6 us
  transfers between devices with their start and end apart: 3, of which 3 were waited for; matrix products, arithmetic and copies ran while one was open for 0% of the time, Pallas kernels for 0%

commit v1 on v0

v1 whole, which is shorter than its diff:
```python
import jax
import jax.numpy as jnp
from jax import lax
from jax.experimental import pallas as pl
from jax.experimental.pallas import tpu as pltpu
from jax.sharding import PartitionSpec as P

MESH = pl.DeviceIdType.MESH
F32, BF16 = jnp.float32, jnp.bfloat16
HIGH = lax.Precision.HIGHEST
NN = (((1,), (0,)), ((), ()))
NT = (((1,), (1,)), ((), ()))

ACTS, A_RS, A_AG, S_RS, S_EX, S_AG, B_RS, B_AG, S_ALL, F_CORE, F_RS, F_AG, F_OUT = range(13)
STAGES = 13

PLANE = sorted(
    [(a, b) for a in range(4) for b in range(4) if a or b],
    key=lambda p: -(min(p[0], 4 - p[0]) + min(p[1], 4 - p[1])),
)


def two_parts(value):
    high = value.astype(BF16)
    low = (value - high.astype(F32)).astype(BF16)
    return jnp.concatenate([high, low], axis=0)


def dot_parts(left, right, dims):
    both = lax.dot_general(two_parts(left), right, dims, preferred_element_type=F32)
    rows = left.shape[0]
    return both[:rows] + both[rows:]


def add_up(ref, count):
    total = ref[0]
    for i in range(1, count):
        total = total + ref[i]
    return total


def inverse_factor(gram):
    n = gram.shape[0]
    row = lax.broadcasted_iota(jnp.int32, (n, 1), 0)
    eye = lax.broadcasted_iota(jnp.int32, (n, n), 0) == lax.broadcasted_iota(jnp.int32, (n, n), 1)
    m = jnp.concatenate([gram, jnp.where(eye, 1.0, 0.0).astype(F32)], axis=1)
    for j in range(n - 1):
        scale = jnp.where(row > j, m[:, j : j + 1] / m[j : j + 1, j : j + 1], 0.0)
        m = m - scale * m[j : j + 1, :]
    pivots = jnp.sum(jnp.where(eye, m[:, :n], 0.0), axis=1, keepdims=True)
    return m[:, n:] * (1.0 / jnp.sqrt(pivots))


def kernel(
    acts, og, q, basis, factor,
    ac, a_part, a_recv, a_tot, a_full,
    s_part, s_recv, s_red, s_b, s_tot, s_full,
    b_part, b_recv, b_tot, b_full, s_all,
    f_part, f_core, f_half, f_recv, f_tot, f_all,
    ssem, rsem,
):
    dp, te = lax.axis_index("dp"), lax.axis_index("tensor")
    z, c = lax.div(dp, 2), lax.rem(dp, 2)
    y, x = lax.div(te, 4), lax.rem(te, 4)
    mate = 2 * z + 1 - c
    group, g = lax.div(dp, 8), lax.rem(dp, 8)
    plane = [lax.rem(y + a, 4) * 4 + lax.rem(x + b, 4) for a, b in PLANE]
    near = [lax.rem(g + j, 8) for j in range(1, 8)]

    def send(src, dst, stage, to):
        pltpu.make_async_remote_copy(
            src_ref=src, dst_ref=dst, send_sem=ssem.at[stage], recv_sem=rsem.at[stage],
            device_id=to, device_id_type=MESH,
        ).start()

    def arrived(ref, stage):
        pltpu.make_async_copy(ref, ref, rsem.at[stage]).wait()

    def sent(ref, stage):
        pltpu.make_async_copy(ref, ref, ssem.at[stage]).wait()

    barrier = pltpu.get_barrier_semaphore()
    for t in plane:
        pl.semaphore_signal(barrier, inc=1, device_id=(dp, t), device_id_type=MESH)

    def greet(j, carry):
        pl.semaphore_signal(barrier, inc=1, device_id=(lax.rem(dp + 2 * j, 64), te), device_id_type=MESH)
        return carry

    lax.fori_loop(1, 32, greet, 0)
    for j in range(4):
        pl.semaphore_signal(barrier, inc=1, device_id=(8 * group + 2 * j + 1 - c, te), device_id_type=MESH)

    def to_tiles(value, part):
        for p in range(16):
            part[p] = value[8 * (p // 2) : 8 * (p // 2) + 8, 128 * (p % 2) : 128 * (p % 2) + 128]

    def from_tiles(full):
        return jnp.concatenate(
            [jnp.concatenate([full[2 * k], full[2 * k + 1]], axis=1) for k in range(8)], axis=0
        )

    def plane_scatter(part, recv, stage):
        for t in plane:
            send(part.at[t], recv.at[te], stage, (dp, t))

    def plane_sum(part, recv, tot, full, stage):
        recv[te] = part[te]
        arrived(recv.at[pl.ds(0, 15)], stage)
        total = add_up(recv, 16)
        tot[...] = total
        full[te] = total
        for t in plane:
            send(tot, full.at[te], stage + 1, (dp, t))

    to_tiles(lax.dot_general(q[...], og[...], NT, preferred_element_type=F32), a_part)
    own_cols = pl.ds(pl.multiple_of(te * 256, 256), 256)
    own_rows = pl.ds(pl.multiple_of(te * 16, 16), 16)
    ac[own_rows, :] = acts[:, own_cols]

    pl.semaphore_wait(barrier, 15 + 31 + 4)

    plane_scatter(a_part, a_recv, A_RS)
    for t in plane:
        send(acts.at[:, pl.ds(pl.multiple_of(t * 256, 256), 256)], ac.at[own_rows, :], ACTS, (dp, t))
    plane_sum(a_part, a_recv, a_tot, a_full, A_RS)
    arrived(ac.at[pl.ds(0, 240), :], ACTS)
    arrived(a_full.at[pl.ds(0, 15)], A_AG)

    left = dot_parts(from_tiles(a_full), ac[...], NN)
    for k in range(8):
        s_part[k] = left[8 * k : 8 * k + 8, :]
    for m in near:
        send(s_part.at[m], s_recv.at[g], S_RS, (8 * group + m, te))
    s_recv[g] = s_part[g]
    arrived(s_recv.at[pl.ds(0, 7)], S_RS)
    s_red[...] = add_up(s_recv, 8)
    for j in (4, 3, 5, 2, 6, 1, 7):
        send(s_red, s_b.at[group], S_EX, (lax.rem(dp + 8 * j, 64), te))
    s_b[group] = s_red[...]
    arrived(s_b.at[pl.ds(0, 7)], S_EX)
    total = add_up(s_b, 8)
    s_tot[...] = total
    s_full[g] = total
    for m in near:
        send(s_tot, s_full.at[g], S_AG, (8 * group + m, te))
    arrived(s_full.at[pl.ds(0, 7)], S_AG)
    summed = jnp.concatenate([s_full[k] for k in range(8)], axis=0)

    to_tiles(dot_parts(summed, ac[...], NT), b_part)
    plane_scatter(b_part, b_recv, B_RS)
    s_all[te] = summed
    plane_sum(b_part, b_recv, b_tot, b_full, B_RS)
    for t in plane:
        send(s_all.at[te], s_all.at[te], S_ALL, (dp, t))
    arrived(b_full.at[pl.ds(0, 15)], B_AG)

    raw = dot_parts(from_tiles(b_full), og[...], NN)
    for p in range(64):
        h, r, k = p // 32, p % 32 // 8, p % 8
        f_part[h, 8 * r + k] = raw[32 * h + 8 * r : 32 * h + 8 * r + 8, 128 * k : 128 * k + 128]
    send(f_part.at[1 - c], f_core, F_CORE, (mate, te))
    arrived(f_core, F_CORE)
    f_half[...] = f_part[c] + f_core[...]

    def ring(i):
        k = lax.div(i + 1, 2)
        return lax.rem(z + 16 + k - 2 * k * (1 - lax.rem(i, 2)), 32)

    def ring_scatter(i, carry):
        to = ring(i)
        send(f_half.at[to], f_recv.at[z], F_RS, (2 * to + c, te))
        return carry

    def ring_gather(i, carry):
        send(f_tot, f_all.at[c, z], F_AG, (2 * ring(i) + c, te))
        return carry

    lax.fori_loop(0, 31, ring_scatter, 0)
    f_recv[z] = f_half[z]
    arrived(f_recv.at[pl.ds(0, 31)], F_RS)
    total = add_up(f_recv, 32)
    f_tot[...] = total
    f_all[c, z] = total
    lax.fori_loop(0, 31, ring_gather, 0)

    arrived(s_all.at[pl.ds(0, 15)], S_ALL)

    def gram_term(t, carry):
        block = s_all[t]
        return carry + lax.dot_general(block, block, NT, precision=HIGH, preferred_element_type=F32)

    inverse = inverse_factor(lax.fori_loop(0, 16, gram_term, jnp.zeros((64, 64), F32)))

    def basis_block(t, carry):
        cols = pl.ds(pl.multiple_of(t * 256, 256), 256)
        basis[:, cols] = lax.dot_general(inverse, s_all[t], NN, precision=HIGH, preferred_element_type=F32)
        return carry

    lax.fori_loop(0, 16, basis_block, 0)

    arrived(f_all.at[c, pl.ds(0, 31)], F_AG)
    send(f_all.at[c], f_all.at[c], F_OUT, (mate, te))
    arrived(f_core, F_OUT)
    mean = inverse * (1.0 / 64)
    for k in range(8):
        tall = jnp.concatenate([f_all[p // 4, 8 * (p % 4) + k] for p in range(8)], axis=0)
        factor[:, 128 * k : 128 * k + 128] = lax.dot_general(
            mean, tall, NN, precision=HIGH, preferred_element_type=F32
        )

    sent(ac.at[pl.ds(0, 240), :], ACTS)
    sent(a_full.at[pl.ds(0, 15)], A_RS)
    sent(a_full.at[pl.ds(0, 15)], A_AG)
    sent(s_full.at[pl.ds(0, 7)], S_RS)
    sent(s_full.at[pl.ds(0, 7)], S_EX)
    sent(s_full.at[pl.ds(0, 7)], S_AG)
    sent(b_full.at[pl.ds(0, 15)], B_RS)
    sent(b_full.at[pl.ds(0, 15)], B_AG)
    sent(s_all.at[pl.ds(0, 15)], S_ALL)
    sent(f_core, F_CORE)
    sent(f_recv.at[pl.ds(0, 31)], F_RS)
    sent(f_recv.at[pl.ds(0, 31)], F_AG)
    sent(f_core, F_OUT)


def shards(acts, out_grad, q_prev):
    vmem = pl.BlockSpec(memory_space=pltpu.VMEM)
    tiles = pltpu.VMEM((16, 8, 128), F32)
    rows = pltpu.VMEM((8, 8, 256), F32)
    one_tile, one_row = pltpu.VMEM((8, 128), F32), pltpu.VMEM((8, 256), F32)
    half = pltpu.VMEM((32, 8, 128), F32)
    return pl.pallas_call(
        kernel,
        out_shape=(jax.ShapeDtypeStruct((64, 4096), F32), jax.ShapeDtypeStruct((64, 1024), F32)),
        in_specs=[vmem] * 3,
        out_specs=(vmem, vmem),
        scratch_shapes=[
            pltpu.VMEM((256, 256), BF16), tiles, tiles, one_tile, tiles,
            rows, rows, one_row, rows, one_row, rows,
            tiles, tiles, one_tile, tiles, pltpu.VMEM((16, 64, 256), F32),
            pltpu.VMEM((2, 32, 8, 128), F32), half, half, half, one_tile, pltpu.VMEM((2, 32, 8, 128), F32),
            pltpu.SemaphoreType.DMA((STAGES,)), pltpu.SemaphoreType.DMA((STAGES,)),
        ],
        compiler_params=pltpu.CompilerParams(
            collective_id=0, has_side_effects=True, vmem_limit_bytes=32 * 1024 * 1024
        ),
        name="powersgd",
    )(acts, out_grad, q_prev)


def solution(mesh):
    in_specs = (P(("dp", "tensor"), None), P("dp", "tensor"), P(None, "tensor"))
    out_specs = (P(), P(None, "tensor"))
    return jax.shard_map(shards, mesh=mesh, in_specs=in_specs, out_specs=out_specs, check_vma=False)
```

time: 1410 us -> 118 us (0.08)
  waiting for transfers between devices: 1360 us -> 0 us
  Pallas kernels: 0 us -> 113 us
  matrix products: 18.6 us -> 0 us
    psum x2 -> x0, waiting for transfers between devices: 1270 us -> none  [the longest x1 892 us: shards(): summed = lax.psum(left_term, ('dp', 'tensor'))]
    pallas_call x0 -> x1, Pallas kernels: none -> 113 us  [shards(): pl.pallas_call(kernel, out_shape=(jax.ShapeDtypeStruct((64, 4096), F32),...]
    all_gather x1 -> x0, waiting for transfers between devices: 92.6 us -> none  [shards(): lax.all_gather(acts, 'tensor', axis=0, tiled=True)]
    dot_general x4 -> x0, matrix products: 16.3 us -> none  [the longest x1 6.03 us: shards(): right_term = jnp.dot(low, grads, preferred_element_type=jnp.float32)]
  transfers between devices with their start and end apart: 3 -> 0, of which waited for: 3 -> 0; matrix products, arithmetic and copies ran while one was open for 0% -> 0% of each run, Pallas kernels for 0% -> 0%
where the time goes in v1:
time: 118 us
  Pallas kernels  113 us (96%)
  local copies, waits for them, and re-layouts  4.52 us (4%)
    pallas_call x1, Pallas kernels, shards(): pl.pallas_call(kernel, out_shape=(jax.ShapeDtypeStruct((64, 4096), F32),...  113 us
    unnamed x8, local copies, waits for them, and re-layouts  4.52 us

profile of v1, /device:TPU:1, one launch (start us, length us, event | category | flops | bytes accessed | tf_op | source)
XLA Modules:
  0.0 117.9 jit_solution(18272735876286738272)
XLA Ops:
  0.6 0.0 copy-start
  0.6 1.0 copy-done
  1.7 0.0 copy-start.1
  1.7 0.9 copy-done.1
  2.6 0.0 copy-start.2
  2.6 0.9 copy-done.2
  3.5 112.7 %powersgd.1 = (f32[64,4096]{1,0:T(8,128)S(1)}, f32[64,1024]{1,0:T(8,128)S(1)}) custom-call(bf16[16,4096]{1,0:T(8,128)(2,1)S(1)} %copy-done.1, bf16[256,1024]{1,0:T(8,128)(2,1)S(1)} %copy-done, bf16[64,1024]{1,0:T(8,128)(2,1)S(1)} %copy-done.2), custom_call_target="tpu_custom_call" | custom-call | tf_op jit(solution)/shard_map/powersgd/pallas_call | solution.py:233
  116.2 1.0 copy.7
  117.2 0.7 copy.8
Async XLA Ops:
  0.6 1.0 copy-start
  1.7 0.9 copy-start.1
  2.6 0.9 copy-start.2
